TPU v7x, 256 devices: a whole 4x4x8 slice. The times are simulated.
256 devices in a mesh: va: 8 (over z_hi, y), vb: 4 (over z_lo), oj: 8 (over x, core).
Axes of the slice: x: 4, y: 4, z: 8 (z_hi: 2, z_lo: 4; z = z_hi * 4 + z_lo), core: 2. Of those that a mesh axis runs over, the one named last changes fastest.
Arguments:
- occ_slab: bfloat16 [3584, 2, 2048], P(('vb', 'oj'), None, 'va'), may hold values from -0.875 to 0.875
- pair_slab: bfloat16 [3584, 8, 2048], P(('va', 'oj'), None, 'vb'), may hold values from -0.875 to 0.875
- occ_energy: float32 [2], replicated, may hold values from -1.5 to -0.3
- pair_energy: float32 [8], P('oj'), may hold values from -1.5 to -0.3
- vir_energy: float32 [2048], replicated, may hold values from 0.2 to 3
Outputs:
- gamma_occ: float32 [3584, 2, 2048], P(('vb', 'oj'), None, 'va')
- gamma_pair: float32 [3584, 8, 2048], P('va', 'oj', 'vb')
All inputs are finite; a program needn't handle non-finite values.
Results may differ from a plain program's by a relative error of at most 0.002.
Values may be sent and summed in bfloat16 or wider, within the bound.
A program may use at most 128 MiB of HBM per device.

v0:
```python
import jax
import jax.numpy as jnp
from jax import lax
from jax.sharding import PartitionSpec as P


def per_device(occ_slab, pair_slab, occ_energy, pair_energy, vir_energy):
    occ_full = lax.all_gather(occ_slab, ("vb", "oj"), axis=0, tiled=True)
    collected = lax.all_gather(pair_slab, "va", axis=0, tiled=True)
    mingled = lax.all_to_all(collected, "oj", split_axis=1, concat_axis=0, tiled=True)
    va_count = lax.axis_size("va")
    oj_count = lax.axis_size("oj")
    shaped = mingled.reshape(oj_count, va_count, -1, mingled.shape[1], mingled.shape[2])
    pair_full = jnp.swapaxes(shaped, 0, 1).reshape(-1, mingled.shape[1], mingled.shape[2])
    width_a = occ_full.shape[2]
    width_b = pair_full.shape[2]
    energy_a = lax.dynamic_slice_in_dim(vir_energy, lax.axis_index("va") * width_a, width_a)
    energy_b = lax.dynamic_slice_in_dim(vir_energy, lax.axis_index("vb") * width_b, width_b)
    pair_ints = jnp.einsum("qia,qjb->ijab", occ_full, pair_full, preferred_element_type=jnp.float32)
    denominator = (
        occ_energy[:, None, None, None]
        + pair_energy[None, :, None, None]
        - energy_a[None, None, :, None]
        - energy_b[None, None, None, :]
    )
    amplitudes = (pair_ints / denominator).astype(jnp.bfloat16)
    gamma_occ = lax.psum_scatter(
        jnp.einsum("ijab,qjb->qia", amplitudes, pair_full, preferred_element_type=jnp.float32),
        ("vb", "oj"),
        scatter_dimension=0,
        tiled=True,
    )
    gamma_pair = lax.psum_scatter(
        jnp.einsum("ijab,qia->qjb", amplitudes, occ_full, preferred_element_type=jnp.float32),
        "va",
        scatter_dimension=0,
        tiled=True,
    )
    return (gamma_occ, gamma_pair)


def solution(mesh):
    placed = (P(("vb", "oj"), None, "va"), P(("va", "oj"), None, "vb"), P(), P("oj"), P())
    return jax.shard_map(
        per_device,
        mesh=mesh,
        in_specs=placed,
        out_specs=(P(("vb", "oj"), None, "va"), P("va", "oj", "vb")),
        check_vma=False,
    )
```

profile of v0, /device:TPU:1, one launch (start us, length us, event | category | flops | bytes accessed | tf_op | source)
XLA Modules:
  0.0 833.1 jit_solution(16251034097933430811)
XLA Ops:
  7.2 0.0 all-gather.3.cloned.1.call-start
  7.2 1.9 copy.25
  9.1 0.0 all-gather.3.cloned.1.call-update
  9.2 0.0 all-gather.5.cloned.1.call-start
  9.2 1.6 copy.27
  10.8 0.0 all-gather.5.cloned.1.call-update
  10.8 0.0 copy-start.1
  10.8 103.1 %all-gather.3.cloned.1.call-done = bf16[448,8,512]{2,0,1:T(8,128)(2,1)} async-done(((bf16[56,8,512]{2,0,1:T(8,128)(2,1)}), bf16[448,8,512]{2,0,1:T(8,128)(2,1)}) %all-gather.3.cloned.1.call-update) | async-done | bytes 3670032 | tf_op jit(solution)/shard_map/all_gather | solution.py:9
  113.9 5.5 all-to-all-start
  119.4 0.0 all-reduce.7.cloned.1.call-start
  120.1 0.8 dynamic_slice.6
  120.8 0.8 dynamic_slice.7
  121.6 0.0 copy-done.1
  121.6 0.1 broadcast_subtract_fusion
  121.7 55.0 %all-to-all-done = bf16[448,8,512]{2,0,1:T(8,128)(2,1)} async-done(((bf16[448,8,512]{2,0,1:T(8,128)(2,1)}), bf16[448,8,512]{2,0,1:T(8,128)(2,1)}, u32[]{:S(2)}, u32[]{:S(2)}) %all-to-all-start) | async-done | bytes 3670048 | tf_op jit(solution)/shard_map/all_to_all | solution.py:10
  176.7 4.2 copy.26
  180.9 11.5 %all-gather.5.cloned.1.call-done = bf16[3584,2,256]{2,0,1:T(8,128)(2,1)} async-done(((bf16[112,2,256]{2,0,1:T(8,128)(2,1)}), bf16[3584,2,256]{2,0,1:T(8,128)(2,1)}) %all-gather.5.cloned.1.call-update) | async-done | bytes 3670032 | tf_op jit(solution)/shard_map/all_gather | solution.py:8
  192.5 0.0 copy-start
  192.5 5.4 fusion.2
  197.9 0.0 copy-done
  197.9 5.1 convolution_bitcast_fusion
  203.0 16.6 %copy.31 = f32[3584,1,512]{2,1,0:T(1,128)} copy(f32[3584,1,512]{0,2,1:T(8,128)} %convolution_bitcast_fusion) | data formatting | bytes 14680064 | tf_op jit(solution)/shard_map/ijab,qia->qjb/dot_general | solution.py:34
  219.6 0.0 all-reduce.7.cloned.1.call-update
  219.7 0.0 all-reduce.5.cloned.1.call-start
  219.7 7.1 convolution_bitcast_fusion.1
  226.8 11.7 %copy.30 = f32[3584,2,256]{2,1,0:T(2,128)} copy(f32[3584,2,256]{0,2,1:T(8,128)} %convolution_bitcast_fusion.1) | data formatting | bytes 14680064 | tf_op jit(solution)/shard_map/ijab,qjb->qia/dot_general | solution.py:28
  238.6 0.0 copy-start.3
  238.6 0.0 copy-start.2
  238.6 0.0 all-reduce.5.cloned.1.call-update
  238.6 0.6 copy-done.3
  239.2 0.6 dynamic-slice.2
  239.8 0.0 copy-done.2
  239.8 0.6 dynamic-slice
  241.7 289.5 %all-reduce.7.cloned.1.call-done = f32[3584,1,512]{2,1,0:T(1,128)} async-done(((f32[3584,1,512]{2,1,0:T(1,128)}), f32[3584,1,512]{2,1,0:T(1,128)}) %all-reduce.7.cloned.1.call-update) | async-done | bytes 7340048
  531.2 2.7 constant_dynamic-slice_fusion
  533.9 291.0 %all-reduce.5.cloned.1.call-done = f32[3584,2,256]{2,1,0:T(2,128)} async-done(((f32[3584,2,256]{2,1,0:T(2,128)}), f32[3584,2,256]{2,1,0:T(2,128)}) %all-reduce.5.cloned.1.call-update) | async-done | bytes 7340048
  824.9 1.6 constant_dynamic-slice_fusion.1
  (1 shorter events, 0.0 us)
Async XLA Ops:
  7.2 106.8 %all-gather.3.cloned.1.call-start = ((), (), s32[]{:S(2)}) async-start(), calls=%async_computation.1 | async-start | bytes 4128768 | tf_op jit(solution)/shard_map/all_gather | solution.py:9
  9.2 183.3 %all-gather.5.cloned.1.call-start = ((), (), s32[]{:S(2)}) async-start(), calls=%async_computation.2 | async-start | bytes 3784704 | tf_op jit(solution)/shard_map/all_gather | solution.py:8
  10.8 110.8 %copy-start.1 = (f32[2]{0:T(128)S(1)}, f32[2]{0:T(128)}, u32[]{:S(2)}) copy-start(f32[2]{0:T(128)} %param.7) | copy-start | bytes 28
  113.9 62.8 %all-to-all-start = ((bf16[448,8,512]{2,0,1:T(8,128)(2,1)}), bf16[448,8,512]{2,0,1:T(8,128)(2,1)}, u32[]{:S(2)}, u32[]{:S(2)}) async-start(bf16[448,8,512]{2,0,1:T(8,128)(2,1)} %all-gather.3.cloned.1.call-done), calls=%async_computation | async-start | bytes 7340032 | tf_op jit(solution)/shard_map/all_to_all | solution.py:10
  119.4 411.8 %all-reduce.7.cloned.1.call-start = ((), (), s32[]{:S(2)}) async-start(), calls=%async_computation.4 | async-start | bytes 14680064
  192.5 5.4 copy-start
  219.7 605.3 %all-reduce.5.cloned.1.call-start = ((), (), s32[]{:S(2)}) async-start(), calls=%async_computation.3 | async-start | bytes 14680064
  238.6 0.7 copy-start.3
  238.6 1.3 copy-start.2
Sparse Core Ops, SparseCore 0:
  11.1 102.7 all-gather.2
  116.3 76.1 all-gather.4
  219.8 311.3 all-reduce.6
  533.7 291.1 all-reduce.4
where the time goes:
time: 834 us; the launch traced here: 833 us
  waiting for transfers between devices  750 us (90%)
  local copies, waits for them, and re-layouts  43.8 us (5%)
  matrix products  17.6 us (2%)
  between operations  15.7 us (2%)
    unnamed x6, waiting for transfers between devices  581 us
    all_gather x1, waiting for transfers between devices, per_device(): collected = lax.all_gather(pair_slab, 'va', axis=0, tiled=True)  103 us
    all_to_all x1, waiting for transfers between devices, per_device(): lax.all_to_all(collected, 'oj', split_axis=1, concat_axis=0, tiled=True)  55 us
  transfers between devices with their start and end apart: 5, of which 5 were waited for; matrix products, arithmetic and copies ran while one was open for 4% of the time, Pallas kernels for 0%

commit v1 on v0

v1 whole, which is shorter than its diff:
```python
import jax
import jax.numpy as jnp
from jax import lax
from jax.experimental import pallas as pl
from jax.experimental.pallas import tpu as pltpu
from jax.sharding import PartitionSpec as P

MESH = pl.DeviceIdType.MESH
BF = jnp.bfloat16
F32 = jnp.float32
ORDER = (0, 1, 3, 2)
PLUS = (0, 3)


def dot(a, b, ca, cb):
    return lax.dot_general(a, b, (((ca,), (cb,)), ((), ())), preferred_element_type=F32)


class Sems:
    def __init__(self, ref, count):
        self.ref, self.count, self.names = ref, count, {}

    def __getitem__(self, name):
        at = self.names.setdefault(name, len(self.names))
        assert at < self.count
        return self.ref.at[at]


N_SEMS = 160


def kernel(
    occ_ref, pair_ref, eo_ref, ep_ref, vir_ref,
    go_ref, gp_ref,
    stage, pairs, zrelay, occs, ecol, tacc, tb,
    gpf, gps, gr, gl, gf, zs2, zr2,
    hof, hsib, hsibr, hxs, hr, hl, hf, hz,
    send_sem, recv_sem,
):
    va, vb, oj = lax.axis_index("va"), lax.axis_index("vb"), lax.axis_index("oj")
    zh, y = va // 4, va % 4
    x, c = oj // 2, oj % 2
    other_c = 1 - c
    z = zh * 4 + vb
    ssem, rsem = Sems(send_sem, N_SEMS), Sems(recv_sem, N_SEMS)
    started = []

    def at_x(dx, dc=False):
        return {"oj": ((x + dx) % 4) * 2 + (other_c if dc else c)}

    def at_y(dy):
        return {"va": zh * 4 + (y + dy) % 4}

    def at_vb(dz):
        return {"vb": (vb + dz) % 4}

    def at_z(zz):
        zz = zz % 8
        return {"va": (zz // 4) * 4 + y, "vb": zz % 4}

    up2 = z + 2 - 4 * c + 8
    up2_dev = at_z(up2)
    down2_dev = at_z(z - 2 + 4 * c + 8)

    def send(name, src, dst, dev):
        copy = pltpu.make_async_remote_copy(
            src_ref=src, dst_ref=dst, send_sem=ssem[name], recv_sem=rsem[name],
            device_id=dev, device_id_type=MESH,
        )
        copy.start()
        started.append(copy)

    def arrived(name, dst):
        pltpu.make_async_remote_copy(
            src_ref=dst, dst_ref=dst, send_sem=ssem[name], recv_sem=rsem[name],
            device_id=at_x(0, True), device_id_type=MESH,
        ).wait_recv()

    barrier = pltpu.get_barrier_semaphore()
    partners = [at_x(dx, dc) for dx in range(4) for dc in (False, True) if dx or dc]
    partners += [at_vb(1), at_vb(2), at_vb(3), at_y(1), at_y(3), up2_dev, down2_dev]
    for dev in partners:
        pl.semaphore_signal(barrier, inc=1, device_id=dev, device_id_type=MESH)
    pl.semaphore_wait(barrier, len(partners))

    def pblk(h, yy, xx):
        hh = zh if h == 0 else 1 - zh
        return pairs.at[(hh * 4 + yy) * 2 + xx // 2, xx % 2]

    def xs(e):
        return (x + 4 - e) % 4

    def zsrc(f):
        return (vb + 4 - f) % 4

    def oblk(f, dx, sib=False):
        return occs.at[zsrc(f) * 8 + ((x + dx) % 4) * 2 + (other_c if sib else c)]

    for dx, dc in ((0, True), (1, False), (1, True), (3, False), (3, True), (2, False), (2, True)):
        dev = at_x(dx, dc)
        send(("s1", dx, dc), pair_ref.at[dev["oj"]], stage.at[dx * 2 + int(dc)], dev)
    own_rows = occs.at[vb * 8 + oj]
    for f in (1, 3, 2):
        send(("oz", f), occ_ref, own_rows, at_vb(f))
    own_rows[...] = occ_ref[...]
    stage[0] = pair_ref[oj]

    def occ_spread(f):
        blk = oblk(f, 0)
        send(("oR", f), blk, blk, at_x(1))
        send(("oL", f), blk, blk, at_x(3))
        send(("oS", 0, f), blk, blk, at_x(0, True))

    def pair_merge(e):
        if e == 0:
            arrived(("s1", 0, True), stage.at[1])
        else:
            for dc in (False, True):
                arrived(("s1", e, dc), stage.at[e * 2 + int(dc)])
        low = stage[e * 2 + c].astype(F32)
        high = stage[e * 2 + other_c].astype(F32)
        blk = pblk(0, y, xs(e))
        blk[...] = jnp.concatenate([low, high], axis=0).astype(BF)
        send(("zr", e), blk, zrelay.at[e], up2_dev)
        pair_spread(0, e)

    def pair_spread(h, e):
        blk = pblk(h, y, xs(e))
        send(("yR", h, e), blk, blk, at_y(1))
        send(("yL", h, e), blk, blk, at_y(3))

    pair_merge(0)
    occ_spread(0)
    pair_merge(1)
    pair_merge(3)
    pair_merge(2)

    va_row = vir_ref[:, pl.ds(pl.multiple_of(va * 256, 256), 256)]
    ecol[...] = jnp.broadcast_to(va_row, (128, 256)).T
    tacc[...] = jnp.zeros_like(tacc)

    for f in (1, 3, 2):
        arrived(("oz", f), oblk(f, 0))
        occ_spread(f)

    zorig = ((z - 2 + 4 * c + 8) % 8) // 4

    def z_forward(e):
        arrived(("zr", e), zrelay.at[e])
        dst = pairs.at[(zorig * 4 + y) * 2 + xs(e) // 2, xs(e) % 2]
        send(("zf", e), zrelay.at[e], dst, up2_dev)

    def y_forward(h, e):
        right = pblk(h, (y + 3) % 4, xs(e))
        left = pblk(h, (y + 1) % 4, xs(e))
        if e in PLUS:
            arrived(("yR", h, e), right)
            send(("yF", h, e), right, right, at_y(1))
            arrived(("yL", h, e), left)
        else:
            arrived(("yL", h, e), left)
            send(("yF", h, e), left, left, at_y(3))
            arrived(("yR", h, e), right)

    def occ_forward(f):
        right, left = oblk(f, 3), oblk(f, 1)
        arrived(("oR", f), right)
        if f in PLUS:
            send(("oF", f), right, right, at_x(1))
        send(("oS", 1, f), right, right, at_x(0, True))
        arrived(("oL", f), left)
        if f not in PLUS:
            send(("oF", f), left, left, at_x(3))
        send(("oS", 2, f), left, left, at_x(0, True))

    for e in ORDER:
        z_forward(e)
        y_forward(0, e)
        occ_forward(e)
    for e in ORDER:
        arrived(("zf", e), pblk(1, y, xs(e)))
        pair_spread(1, e)
    for f in ORDER:
        far = oblk(f, 2)
        arrived(("oF", f), far)
        send(("oS", 3, f), far, far, at_x(0, True))
    for f in ORDER:
        for m, dx in ((0, 0), (1, 3), (2, 1), (3, 2)):
            arrived(("oS", m, f), oblk(f, dx, True))

    def t_add(h, dy):
        hh = zh if h == 0 else 1 - zh
        group = hh * 4 + (y + dy) % 4
        a = occs[pl.ds(group * 4, 4)].reshape(448, 512)
        b = pairs[pl.ds(group * 2, 2)].reshape(448, 512)
        tacc[...] += dot(a, b, 0, 0)

    t_add(0, 0)
    t_add(0, 1)
    t_add(0, 3)
    t_add(1, 0)
    for e in ORDER:
        y_forward(1, e)
    t_add(1, 1)
    t_add(1, 3)
    for e in ORDER:
        arrived(("yF", 0, e), pblk(0, (y + 2) % 4, xs(e)))
    t_add(0, 2)
    for e in ORDER:
        arrived(("yF", 1, e), pblk(1, (y + 2) % 4, xs(e)))
    t_add(1, 2)

    vb_row = vir_ref[:, pl.ds(pl.multiple_of(vb * 512, 512), 512)]
    va_cols = jnp.concatenate([ecol[...]] * 4, axis=1)
    for i in range(2):
        den = ((eo_ref[i] + ep_ref[0]) - va_cols) - vb_row
        tb[i * 256:(i + 1) * 256] = (tacc[i * 256:(i + 1) * 256] / den).astype(BF)

    def g_block(h, dy):
        hh = zh if h == 0 else 1 - zh
        group = hh * 4 + (y + dy) % 4
        rows = occs[pl.ds(group * 4, 4)].reshape(448, 512)
        gpf[h, dy] = dot(rows, tb[...], 1, 0).reshape(4, 112, 512)

    def g_direct(h, dy, t, name, dev, dst):
        gps[h, dy, t] = gpf[h, dy, t].astype(BF)
        send((name, h, t), gps.at[h, dy, t], dst.at[h, t], dev)

    def g_start(h):
        g_block(h, 2)
        for t in range(4):
            g_direct(h, 2, t, "gF", at_y(1 if t in PLUS else 3), gf)
        g_block(h, 1)
        g_block(h, 3)
        for t in range(4):
            if t in PLUS:
                g_direct(h, 3, t, "gL", at_y(3), gl)
            else:
                g_direct(h, 1, t, "gR", at_y(1), gr)

    def g_relay(h):
        for t in range(4):
            arrived(("gF", h, t), gf.at[h, t])
            dy = 1 if t in PLUS else 3
            gps[h, dy, t] = (gpf[h, dy, t] + gf[h, t].astype(F32)).astype(BF)
            if t in PLUS:
                send(("gR", h, t), gps.at[h, dy, t], gr.at[h, t], at_y(1))
            else:
                send(("gL", h, t), gps.at[h, dy, t], gl.at[h, t], at_y(3))

    def g_sum(h, t):
        arrived(("gR", h, t), gr.at[h, t])
        arrived(("gL", h, t), gl.at[h, t])
        return gpf[h, 0, t] + gr[h, t].astype(F32) + gl[h, t].astype(F32)

    def h_block(f):
        group = (vb + f) % 4
        rows = pairs[pl.ds(group * 4, 4), other_c].reshape(448, 512)
        hsib[f] = dot(rows, tb[...], 1, 1).astype(BF).reshape(4, 112, 512)
        send(("hS", f), hsib.at[f], hsibr.at[f], at_x(0, True))
        rows = pairs[pl.ds(group * 4, 4), c].reshape(448, 512)
        hof[f] = dot(rows, tb[...], 1, 1).reshape(4, 112, 512)

    def h_start(f):
        arrived(("hS", f), hsibr.at[f])
        hof[f] += hsibr[f].astype(F32)
        hxs[f, 2] = hof[f, (x + 2) % 4].astype(BF)
        send(("hF", f), hxs.at[f, 2], hf.at[f], at_x(1 if f in PLUS else 3))
        if f in PLUS:
            hxs[f, 3] = hof[f, (x + 3) % 4].astype(BF)
            send(("hL", f), hxs.at[f, 3], hl.at[f], at_x(3))
        else:
            hxs[f, 1] = hof[f, (x + 1) % 4].astype(BF)
            send(("hR", f), hxs.at[f, 1], hr.at[f], at_x(1))

    def h_relay(f):
        arrived(("hF", f), hf.at[f])
        dx = 1 if f in PLUS else 3
        hxs[f, dx] = (hof[f, (x + dx) % 4] + hf[f].astype(F32)).astype(BF)
        if f in PLUS:
            send(("hR", f), hxs.at[f, dx], hr.at[f], at_x(1))
        else:
            send(("hL", f), hxs.at[f, dx], hl.at[f], at_x(3))

    def h_sum(f):
        arrived(("hR", f), hr.at[f])
        arrived(("hL", f), hl.at[f])
        return hof[f, x] + hr[f].astype(F32) + hl[f].astype(F32)

    def h_finish(f):
        hxs[f, 0] = h_sum(f).astype(BF)
        send(("hz", f), hxs.at[f, 0], hz.at[f], at_vb(f))

    g_start(1)
    g_start(0)
    h_block(2)
    h_block(1)
    g_relay(1)
    h_start(2)
    h_start(1)
    h_block(3)
    h_block(0)
    h_start(3)
    h_start(0)
    g_block(1, 0)
    g_block(0, 0)
    h_relay(2)
    h_relay(1)
    h_relay(3)
    h_relay(0)
    for t in range(4):
        gps[1, 0, t] = g_sum(1, t).astype(BF)
        send(("z2", t), gps.at[1, 0, t], zr2.at[t], up2_dev)
    h_finish(2)
    h_finish(1)
    h_finish(3)
    g_relay(0)
    for t in range(4):
        arrived(("z2", t), zr2.at[t])
        send(("z3", t), zr2.at[t], zs2.at[t], up2_dev)
    total = h_sum(0)
    for f in (1, 3, 2):
        arrived(("hz", f), hz.at[f])
        total = total + hz[f].astype(F32)
    go_ref[...] = total
    for t in range(4):
        part = g_sum(0, t)
        arrived(("z3", t), zs2.at[t])
        gp_ref[t] = part + zs2[t].astype(F32)
    for copy in started:
        copy.wait_send()


def per_device(occ_slab, pair_slab, occ_energy, pair_energy, vir_energy):
    vmem = pl.BlockSpec(memory_space=pltpu.VMEM)
    smem = pl.BlockSpec(memory_space=pltpu.SMEM)
    chunk = (112, 512)
    gamma_occ, gamma_pair = pl.pallas_call(
        kernel,
        out_shape=(jax.ShapeDtypeStruct(chunk, F32), jax.ShapeDtypeStruct((4,) + chunk, F32)),
        in_specs=[vmem, vmem, smem, smem, vmem],
        out_specs=(vmem, vmem),
        scratch_shapes=[
            pltpu.VMEM((8, 56, 512), BF),
            pltpu.VMEM((16, 2) + chunk, BF),
            pltpu.VMEM((4,) + chunk, BF),
            pltpu.VMEM((32,) + chunk, BF),
            pltpu.VMEM((256, 128), F32),
            pltpu.VMEM((512, 512), F32),
            pltpu.VMEM((512, 512), BF),
            pltpu.VMEM((2, 4, 4) + chunk, F32),
            pltpu.VMEM((2, 4, 4) + chunk, BF),
            pltpu.VMEM((2, 4) + chunk, BF),
            pltpu.VMEM((2, 4) + chunk, BF),
            pltpu.VMEM((2, 4) + chunk, BF),
            pltpu.VMEM((4,) + chunk, BF),
            pltpu.VMEM((4,) + chunk, BF),
            pltpu.VMEM((4, 4) + chunk, F32),
            pltpu.VMEM((4, 4) + chunk, BF),
            pltpu.VMEM((4, 4) + chunk, BF),
            pltpu.VMEM((4, 4) + chunk, BF),
            pltpu.VMEM((4,) + chunk, BF),
            pltpu.VMEM((4,) + chunk, BF),
            pltpu.VMEM((4,) + chunk, BF),
            pltpu.VMEM((4,) + chunk, BF),
            pltpu.SemaphoreType.DMA((N_SEMS,)),
            pltpu.SemaphoreType.DMA((N_SEMS,)),
        ],
        compiler_params=pltpu.CompilerParams(
            collective_id=0, has_side_effects=True, vmem_limit_bytes=60 * 1024 * 1024
        ),
        cost_estimate=pl.CostEstimate(flops=5_600_000_000, bytes_accessed=2_000_000, transcendentals=0),
    )(
        occ_slab.reshape(chunk),
        jnp.swapaxes(pair_slab, 0, 1),
        occ_energy,
        pair_energy,
        vir_energy.reshape(1, -1),
    )
    return gamma_occ.reshape(112, 2, 256), gamma_pair.reshape(448, 1, 512)


def solution(mesh):
    placed = (P(("vb", "oj"), None, "va"), P(("va", "oj"), None, "vb"), P(), P("oj"), P())
    return jax.shard_map(
        per_device,
        mesh=mesh,
        in_specs=placed,
        out_specs=(P(("vb", "oj"), None, "va"), P("va", "oj", "vb")),
        check_vma=False,
    )
```

time: 834 us -> 121 us (0.15)
  waiting for transfers between devices: 750 us -> 0 us
  Pallas kernels: 0 us -> 111 us
  local copies, waits for them, and re-layouts: 43.8 us -> 8.29 us
  matrix products: 17.6 us -> 0 us
  between operations: 15.7 us -> 1.29 us
    unnamed x6 -> x0, waiting for transfers between devices: 581 us -> none
    all_gather x2 -> x0, waiting for transfers between devices: 115 us -> none  [the longest x1 103 us: per_device(): collected = lax.all_gather(pair_slab, 'va', axis=0, tiled=True)]
    pallas_call x0 -> x1, Pallas kernels: none -> 111 us  [per_device(): pl.pallas_call(kernel, out_shape=(jax.ShapeDtypeStruct(chunk, F32), jax.S...]
    all_to_all x1 -> x0, waiting for transfers between devices: 55 us -> none  [per_device(): lax.all_to_all(collected, 'oj', split_axis=1, concat_axis=0, tiled=True)]
    dot_general x2 -> x0, local copies, waits for them, and re-layouts: 28.4 us -> none  [the longest x1 16.6 us: per_device(): jnp.einsum('ijab,qia->qjb', amplitudes, occ_full, preferred_element_type=...]
    dot_general x3 -> x0, matrix products: 17.6 us -> none  [the longest x1 7.13 us: per_device(): jnp.einsum('ijab,qjb->qia', amplitudes, pair_full, preferred_element_type...]
  transfers between devices with their start and end apart: 5 -> 0, of which waited for: 5 -> 0; matrix products, arithmetic and copies ran while one was open for 4% -> 0% of each run, Pallas kernels for 0% -> 0%
where the time goes in v1:
time: 121 us
  Pallas kernels  111 us (92%)
  local copies, waits for them, and re-layouts  8.29 us (7%)
  between operations  1.29 us (1%)
    pallas_call x1, Pallas kernels, per_device(): pl.pallas_call(kernel, out_shape=(jax.ShapeDtypeStruct(chunk, F32), jax.S...  111 us
    unnamed x3, local copies, waits for them, and re-layouts  6.52 us

profile of v1, /device:TPU:1, one launch (start us, length us, event | category | flops | bytes accessed | tf_op | source)
XLA Modules:
  0.0 120.6 jit_solution(16928441822471683297)
XLA Ops:
  1.3 1.6 %copy.9 = bf16[14,8,2,256]{3,1,2,0:T(8,128)(2,1)} copy(bf16[14,8,2,256]{3,2,1,0:T(2,128)(2,1)} %bitcast.9) | data formatting | bytes 229376
  2.8 1.9 %copy.11 = bf16[56,8,512]{2,0,1:T(8,128)(2,1)} copy(bf16[56,8,512]{2,1,0:T(8,128)(2,1)} %param.6) | data formatting | bytes 917504 | tf_op args[1]
  4.8 111.0 %shard_map.68 = (f32[112,512]{1,0:T(8,128)}, f32[4,112,512]{2,1,0:T(8,128)}) custom-call(bf16[112,512]{1,0:T(8,128)(2,1)} %bitcast.10, bf16[8,56,512]{2,1,0:T(8,128)(2,1)} %bitcast.8, f32[2]{0:T(128)} %eo_ref.1, f32[1]{0:T(128)S(6)} %copy.12.ep_ref, f32[1,2048]{1,0:T(1,128)} %bitcast.11), custom_call_target="tpu_custom_call" | custom-call | flops 5600000000 | bytes 2000000 | tf_op jit(solution)/shard_map/pallas_call | solution.py:338
  115.8 1.8 %reshape.18 = f32[112,2,256]{2,1,0:T(2,128)} reshape(f32[112,512]{1,0:T(8,128)} %get-tuple-element.4) | data formatting | bytes 458752 | tf_op jit(solution)/shard_map/reshape | solution.py:380
  117.5 3.0 %copy.8 = f32[448,1,512]{2,1,0:T(1,128)} copy(f32[448,1,512]{2,0,1:T(8,128)} %bitcast.7) | data formatting | bytes 1835008

commit v2 on v1

--- a/solution.py
+++ b/solution.py
@@ -129,20 +129,6 @@
         send(("yR", h, e), blk, blk, at_y(1))
         send(("yL", h, e), blk, blk, at_y(3))
 
-    pair_merge(0)
-    occ_spread(0)
-    pair_merge(1)
-    pair_merge(3)
-    pair_merge(2)
-
-    va_row = vir_ref[:, pl.ds(pl.multiple_of(va * 256, 256), 256)]
-    ecol[...] = jnp.broadcast_to(va_row, (128, 256)).T
-    tacc[...] = jnp.zeros_like(tacc)
-
-    for f in (1, 3, 2):
-        arrived(("oz", f), oblk(f, 0))
-        occ_spread(f)
-
     zorig = ((z - 2 + 4 * c + 8) % 8) // 4
 
     def z_forward(e):
@@ -173,17 +159,55 @@
             send(("oF", f), left, left, at_x(3))
         send(("oS", 2, f), left, left, at_x(0, True))
 
-    for e in ORDER:
-        z_forward(e)
-        y_forward(0, e)
-        occ_forward(e)
-    for e in ORDER:
+    va_row = vir_ref[:, pl.ds(pl.multiple_of(va * 256, 256), 256)]
+    ecol[...] = jnp.broadcast_to(va_row, (128, 256)).T
+    tacc[...] = jnp.zeros_like(tacc)
+
+    def occ_in(f):
+        arrived(("oz", f), oblk(f, 0))
+        occ_spread(f)
+
+    def z_in(e):
         arrived(("zf", e), pblk(1, y, xs(e)))
         pair_spread(1, e)
-    for f in ORDER:
+
+    def occ_far(f):
         far = oblk(f, 2)
         arrived(("oF", f), far)
         send(("oS", 3, f), far, far, at_x(0, True))
+
+    pair_merge(0)
+    occ_spread(0)
+    pair_merge(1)
+    pair_merge(3)
+    y_forward(0, 0)
+    pair_merge(2)
+    z_forward(0)
+    y_forward(0, 1)
+    occ_in(1)
+    y_forward(0, 3)
+    z_forward(1)
+    occ_in(3)
+    y_forward(0, 2)
+    z_in(0)
+    occ_in(2)
+    occ_forward(0)
+    z_forward(3)
+    occ_forward(1)
+    z_in(1)
+    y_forward(1, 0)
+    z_forward(2)
+    occ_forward(3)
+    occ_far(0)
+    z_in(3)
+    y_forward(1, 1)
+    occ_forward(2)
+    occ_far(1)
+    z_in(2)
+    y_forward(1, 3)
+    occ_far(3)
+    occ_far(2)
+    y_forward(1, 2)
     for f in ORDER:
         for m, dx in ((0, 0), (1, 3), (2, 1), (3, 2)):
             arrived(("oS", m, f), oblk(f, dx, True))
@@ -200,12 +224,10 @@
     t_add(0, 3)
     t_add(1, 0)
     for e in ORDER:
-        y_forward(1, e)
+        arrived(("yF", 0, e), pblk(0, (y + 2) % 4, xs(e)))
+    t_add(0, 2)
     t_add(1, 1)
     t_add(1, 3)
-    for e in ORDER:
-        arrived(("yF", 0, e), pblk(0, (y + 2) % 4, xs(e)))
-    t_add(0, 2)
     for e in ORDER:
         arrived(("yF", 1, e), pblk(1, (y + 2) % 4, xs(e)))
     t_add(1, 2)
@@ -226,10 +248,12 @@
         gps[h, dy, t] = gpf[h, dy, t].astype(BF)
         send((name, h, t), gps.at[h, dy, t], dst.at[h, t], dev)
 
-    def g_start(h):
+    def g_far(h):
         g_block(h, 2)
         for t in range(4):
             g_direct(h, 2, t, "gF", at_y(1 if t in PLUS else 3), gf)
+
+    def g_near(h):
         g_block(h, 1)
         g_block(h, 3)
         for t in range(4):
@@ -238,8 +262,8 @@
             else:
                 g_direct(h, 1, t, "gR", at_y(1), gr)
 
-    def g_relay(h):
-        for t in range(4):
+    def g_relay(h, ts):
+        for t in ts:
             arrived(("gF", h, t), gf.at[h, t])
             dy = 1 if t in PLUS else 3
             gps[h, dy, t] = (gpf[h, dy, t] + gf[h, t].astype(F32)).astype(BF)
@@ -291,33 +315,45 @@
         hxs[f, 0] = h_sum(f).astype(BF)
         send(("hz", f), hxs.at[f, 0], hz.at[f], at_vb(f))
 
-    g_start(1)
-    g_start(0)
+    def z_out(t):
+        gps[1, 0, t] = g_sum(1, t).astype(BF)
+        send(("z2", t), gps.at[1, 0, t], zr2.at[t], up2_dev)
+
+    def z_pass(t):
+        arrived(("z2", t), zr2.at[t])
+        send(("z3", t), zr2.at[t], zs2.at[t], up2_dev)
+
+    g_far(1)
     h_block(2)
+    g_near(1)
     h_block(1)
-    g_relay(1)
+    h_block(3)
     h_start(2)
     h_start(1)
-    h_block(3)
+    g_relay(1, (0, 1, 2, 3))
+    h_start(3)
+    g_far(0)
     h_block(0)
-    h_start(3)
-    h_start(0)
     g_block(1, 0)
-    g_block(0, 0)
     h_relay(2)
     h_relay(1)
+    g_near(0)
+    z_out(0)
+    z_out(1)
     h_relay(3)
-    h_relay(0)
-    for t in range(4):
-        gps[1, 0, t] = g_sum(1, t).astype(BF)
-        send(("z2", t), gps.at[1, 0, t], zr2.at[t], up2_dev)
+    z_out(2)
+    z_out(3)
     h_finish(2)
     h_finish(1)
+    g_block(0, 0)
+    h_start(0)
     h_finish(3)
-    g_relay(0)
-    for t in range(4):
-        arrived(("z2", t), zr2.at[t])
-        send(("z3", t), zr2.at[t], zs2.at[t], up2_dev)
+    z_pass(0)
+    z_pass(1)
+    g_relay(0, (0, 1, 2, 3))
+    h_relay(0)
+    z_pass(2)
+    z_pass(3)
     total = h_sum(0)
     for f in (1, 3, 2):
         arrived(("hz", f), hz.at[f])

time: 121 us -> 112 us (0.926)
  the two profiles are of different devices: /device:TPU:1 before, /device:TPU:64 now
where the time goes in v2:
time: 112 us
  Pallas kernels  102 us (91%)
  local copies, waits for them, and re-layouts  8.29 us (7%)
  between operations  1.29 us (1%)
    pallas_call x1, Pallas kernels, per_device(): pl.pallas_call(kernel, out_shape=(jax.ShapeDtypeStruct(chunk, F32), jax.S...  102 us
    unnamed x3, local copies, waits for them, and re-layouts  6.52 us

profile of v2, /device:TPU:64, one launch (start us, length us, event | category | flops | bytes accessed | tf_op | source)
XLA Modules:
  0.0 112.0 jit_solution(15256328044739817861)
XLA Ops:
  1.3 1.6 %copy.9 = bf16[14,8,2,256]{3,1,2,0:T(8,128)(2,1)} copy(bf16[14,8,2,256]{3,2,1,0:T(2,128)(2,1)} %bitcast.9) | data formatting | bytes 229376
  2.8 1.9 %copy.11 = bf16[56,8,512]{2,0,1:T(8,128)(2,1)} copy(bf16[56,8,512]{2,1,0:T(8,128)(2,1)} %param.6) | data formatting | bytes 917504 | tf_op args[1]
  4.8 102.4 %shard_map.68 = (f32[112,512]{1,0:T(8,128)}, f32[4,112,512]{2,1,0:T(8,128)}) custom-call(bf16[112,512]{1,0:T(8,128)(2,1)} %bitcast.10, bf16[8,56,512]{2,1,0:T(8,128)(2,1)} %bitcast.8, f32[2]{0:T(128)} %eo_ref.1, f32[1]{0:T(128)S(6)} %copy.12.ep_ref, f32[1,2048]{1,0:T(1,128)} %bitcast.11), custom_call_target="tpu_custom_call" | custom-call | flops 5600000000 | bytes 2000000 | tf_op jit(solution)/shard_map/pallas_call | solution.py:374
  107.2 1.8 %reshape.18 = f32[112,2,256]{2,1,0:T(2,128)} reshape(f32[112,512]{1,0:T(8,128)} %get-tuple-element.4) | data formatting | bytes 458752 | tf_op jit(solution)/shard_map/reshape | solution.py:416
  109.0 3.0 %copy.8 = f32[448,1,512]{2,1,0:T(1,128)} copy(f32[448,1,512]{2,0,1:T(8,128)} %bitcast.7) | data formatting | bytes 1835008

commit v3 on v2

--- a/solution.py
+++ b/solution.py
@@ -9,6 +9,8 @@
 BF = jnp.bfloat16
 F32 = jnp.float32
 ORDER = (0, 1, 3, 2)
+PAIR_DIRECT = ((1, 2),)
+OCC_DIRECT = (3,)
 PLUS = (0, 3)
 
 
@@ -20,20 +22,23 @@
     def __init__(self, ref, count):
         self.ref, self.count, self.names = ref, count, {}
 
-    def __getitem__(self, name):
+    def index(self, name):
         at = self.names.setdefault(name, len(self.names))
         assert at < self.count
-        return self.ref.at[at]
+        return at
+
+    def __getitem__(self, name):
+        return self.ref.at[self.index(name)]
 
 
 N_SEMS = 160
 
 
 def kernel(
-    occ_ref, pair_ref, eo_ref, ep_ref, vir_ref,
+    occ_raw, pair_raw, eo_ref, ep_ref, vir_ref,
     go_ref, gp_ref,
-    stage, pairs, zrelay, occs, ecol, tacc, tb,
-    gpf, gps, gr, gl, gf, zs2, zr2,
+    occ_wide, pair_wide, occ_ref, pair_ref, stage, pairs, occs, ecol, tacc, tb,
+    gpf, gps, gr, gl, gf, zs2,
     hof, hsib, hsibr, hxs, hr, hl, hf, hz,
     send_sem, recv_sem,
 ):
@@ -41,9 +46,8 @@
     zh, y = va // 4, va % 4
     x, c = oj // 2, oj % 2
     other_c = 1 - c
-    z = zh * 4 + vb
     ssem, rsem = Sems(send_sem, N_SEMS), Sems(recv_sem, N_SEMS)
-    started = []
+    started = {}
 
     def at_x(dx, dc=False):
         return {"oj": ((x + dx) % 4) * 2 + (other_c if dc else c)}
@@ -54,21 +58,26 @@
     def at_vb(dz):
         return {"vb": (vb + dz) % 4}
 
-    def at_z(zz):
-        zz = zz % 8
-        return {"va": (zz // 4) * 4 + y, "vb": zz % 4}
-
-    up2 = z + 2 - 4 * c + 8
-    up2_dev = at_z(up2)
-    down2_dev = at_z(z - 2 + 4 * c + 8)
-
-    def send(name, src, dst, dev):
+    across = {"va": (1 - zh) * 4 + y}
+
+    def send(name, src, dst, dev, when=None, recv_name=None):
         copy = pltpu.make_async_remote_copy(
-            src_ref=src, dst_ref=dst, send_sem=ssem[name], recv_sem=rsem[name],
+            src_ref=src, dst_ref=dst, send_sem=ssem[name],
+            recv_sem=rsem[name] if recv_name is None else recv_name,
             device_id=dev, device_id_type=MESH,
         )
-        copy.start()
-        started.append(copy)
+        started[name] = (copy, when)
+        if when is None:
+            copy.start()
+        else:
+            pl.when(when)(copy.start)
+
+    def sent(name):
+        copy, when = started.pop(name)
+        if when is None:
+            copy.wait_send()
+        else:
+            pl.when(when)(copy.wait_send)
 
     def arrived(name, dst):
         pltpu.make_async_remote_copy(
@@ -78,9 +87,16 @@
 
     barrier = pltpu.get_barrier_semaphore()
     partners = [at_x(dx, dc) for dx in range(4) for dc in (False, True) if dx or dc]
-    partners += [at_vb(1), at_vb(2), at_vb(3), at_y(1), at_y(3), up2_dev, down2_dev]
+    partners += [at_vb(1), at_vb(2), at_vb(3), at_y(1), at_y(2), at_y(3), across]
     for dev in partners:
         pl.semaphore_signal(barrier, inc=1, device_id=dev, device_id_type=MESH)
+    for q in range(4):
+        pair_wide[q] = pair_raw[:, :, q * 128:(q + 1) * 128].astype(F32).reshape(448, 128)
+    for j in range(8):
+        for q in range(4):
+            pair_ref[j, :, q * 128:(q + 1) * 128] = pair_wide[q, pl.ds(j, 56, stride=8), :].astype(BF)
+    occ_wide[...] = occ_raw[...].astype(F32)
+    occ_ref[...] = jnp.concatenate([occ_wide[:, 0, :], occ_wide[:, 1, :]], axis=1).astype(BF)
     pl.semaphore_wait(barrier, len(partners))
 
     def pblk(h, yy, xx):
@@ -91,7 +107,8 @@
         return (x + 4 - e) % 4
 
     def zsrc(f):
-        return (vb + 4 - f) % 4
+        step = {0: 0, 1: jnp.where(vb == 0, 3, 1), 2: 2, 3: jnp.where(vb == 0, 1, 3)}[f]
+        return (vb + 4 - step) % 4
 
     def oblk(f, dx, sib=False):
         return occs.at[zsrc(f) * 8 + ((x + dx) % 4) * 2 + (other_c if sib else c)]
@@ -100,8 +117,17 @@
         dev = at_x(dx, dc)
         send(("s1", dx, dc), pair_ref.at[dev["oj"]], stage.at[dx * 2 + int(dc)], dev)
     own_rows = occs.at[vb * 8 + oj]
-    for f in (1, 3, 2):
-        send(("oz", f), occ_ref, own_rows, at_vb(f))
+
+    oz_at = {f: rsem.index(("oz", f)) for f in (1, 2, 3)}
+
+    def occ_out(f):
+        when = {1: vb != 3, 3: vb != 0, 2: None}[f]
+        near, other = oz_at[1], oz_at[3]
+        slot = {1: near, 2: oz_at[2], 3: jnp.where(vb == 1, near, other)}[f]
+        send(("oz", f), occ_ref, own_rows, at_vb(f), when, recv_sem.at[slot])
+
+    occ_out(1)
+    occ_out(3)
     own_rows[...] = occ_ref[...]
     stage[0] = pair_ref[oj]
 
@@ -109,6 +135,8 @@
         blk = oblk(f, 0)
         send(("oR", f), blk, blk, at_x(1))
         send(("oL", f), blk, blk, at_x(3))
+        if f in OCC_DIRECT:
+            send(("oF", f), blk, blk, at_x(2))
         send(("oS", 0, f), blk, blk, at_x(0, True))
 
     def pair_merge(e):
@@ -121,41 +149,42 @@
         high = stage[e * 2 + other_c].astype(F32)
         blk = pblk(0, y, xs(e))
         blk[...] = jnp.concatenate([low, high], axis=0).astype(BF)
-        send(("zr", e), blk, zrelay.at[e], up2_dev)
         pair_spread(0, e)
 
     def pair_spread(h, e):
         blk = pblk(h, y, xs(e))
         send(("yR", h, e), blk, blk, at_y(1))
         send(("yL", h, e), blk, blk, at_y(3))
-
-    zorig = ((z - 2 + 4 * c + 8) % 8) // 4
-
-    def z_forward(e):
-        arrived(("zr", e), zrelay.at[e])
-        dst = pairs.at[(zorig * 4 + y) * 2 + xs(e) // 2, xs(e) % 2]
-        send(("zf", e), zrelay.at[e], dst, up2_dev)
+        if (h, e) in PAIR_DIRECT:
+            send(("yF", h, e), blk, blk, at_y(2))
+
+    def z_out1(e):
+        blk = pblk(0, y, xs(e))
+        send(("zf", e), blk, blk, across)
 
     def y_forward(h, e):
         right = pblk(h, (y + 3) % 4, xs(e))
         left = pblk(h, (y + 1) % 4, xs(e))
+        onward = (h, e) not in PAIR_DIRECT
         if e in PLUS:
             arrived(("yR", h, e), right)
-            send(("yF", h, e), right, right, at_y(1))
+            if onward:
+                send(("yF", h, e), right, right, at_y(1))
             arrived(("yL", h, e), left)
         else:
             arrived(("yL", h, e), left)
-            send(("yF", h, e), left, left, at_y(3))
+            if onward:
+                send(("yF", h, e), left, left, at_y(3))
             arrived(("yR", h, e), right)
 
     def occ_forward(f):
         right, left = oblk(f, 3), oblk(f, 1)
         arrived(("oR", f), right)
-        if f in PLUS:
+        if f in PLUS and f not in OCC_DIRECT:
             send(("oF", f), right, right, at_x(1))
         send(("oS", 1, f), right, right, at_x(0, True))
         arrived(("oL", f), left)
-        if f not in PLUS:
+        if f not in PLUS and f not in OCC_DIRECT:
             send(("oF", f), left, left, at_x(3))
         send(("oS", 2, f), left, left, at_x(0, True))
 
@@ -164,7 +193,12 @@
     tacc[...] = jnp.zeros_like(tacc)
 
     def occ_in(f):
-        arrived(("oz", f), oblk(f, 0))
+        blk = oblk(f, 0)
+        arrived(("oz", f), blk)
+        if f == 2:
+            other = recv_sem.at[oz_at[3]]
+            send(("ozl",), blk, blk, {"vb": 0}, vb == 1, other)
+            send(("ozh",), blk, blk, {"vb": 3}, vb == 2, other)
         occ_spread(f)
 
     def z_in(e):
@@ -176,37 +210,40 @@
         arrived(("oF", f), far)
         send(("oS", 3, f), far, far, at_x(0, True))
 
+    occ_out(2)
     pair_merge(0)
+    z_out1(0)
     occ_spread(0)
     pair_merge(1)
     pair_merge(3)
     y_forward(0, 0)
     pair_merge(2)
-    z_forward(0)
+    occ_in(2)
+    z_out1(1)
     y_forward(0, 1)
     occ_in(1)
+    occ_in(3)
     y_forward(0, 3)
-    z_forward(1)
-    occ_in(3)
+    sent(("zf", 0))
+    z_out1(3)
+    z_in(0)
     y_forward(0, 2)
-    z_in(0)
-    occ_in(2)
     occ_forward(0)
-    z_forward(3)
-    occ_forward(1)
+    sent(("zf", 1))
+    z_out1(2)
     z_in(1)
     y_forward(1, 0)
-    z_forward(2)
+    occ_forward(2)
+    z_in(3)
+    occ_forward(1)
+    occ_far(0)
+    y_forward(1, 1)
+    z_in(2)
     occ_forward(3)
-    occ_far(0)
-    z_in(3)
-    y_forward(1, 1)
-    occ_forward(2)
+    occ_far(2)
+    y_forward(1, 3)
     occ_far(1)
-    z_in(2)
-    y_forward(1, 3)
     occ_far(3)
-    occ_far(2)
     y_forward(1, 2)
     for f in ORDER:
         for m, dx in ((0, 0), (1, 3), (2, 1), (3, 2)):
@@ -248,15 +285,12 @@
         gps[h, dy, t] = gpf[h, dy, t].astype(BF)
         send((name, h, t), gps.at[h, dy, t], dst.at[h, t], dev)
 
-    def g_far(h):
-        g_block(h, 2)
-        for t in range(4):
+    def g_far(h, ts):
+        for t in ts:
             g_direct(h, 2, t, "gF", at_y(1 if t in PLUS else 3), gf)
 
-    def g_near(h):
-        g_block(h, 1)
-        g_block(h, 3)
-        for t in range(4):
+    def g_near(h, ts):
+        for t in ts:
             if t in PLUS:
                 g_direct(h, 3, t, "gL", at_y(3), gl)
             else:
@@ -317,54 +351,80 @@
 
     def z_out(t):
         gps[1, 0, t] = g_sum(1, t).astype(BF)
-        send(("z2", t), gps.at[1, 0, t], zr2.at[t], up2_dev)
-
-    def z_pass(t):
-        arrived(("z2", t), zr2.at[t])
-        send(("z3", t), zr2.at[t], zs2.at[t], up2_dev)
-
-    g_far(1)
+        send(("z2", t), gps.at[1, 0, t], zs2.at[t], across)
+
+    g_block(1, 2)
+    g_far(1, (0,))
+    g_far(1, (1,))
+    g_block(1, 1)
+    g_block(1, 3)
+    g_near(1, (0,))
+    g_near(1, (1,))
     h_block(2)
-    g_near(1)
+    g_far(1, (3,))
+    g_far(1, (2,))
+    g_relay(1, (0,))
+    g_relay(1, (1,))
     h_block(1)
     h_block(3)
+    g_near(1, (3,))
+    g_near(1, (2,))
     h_start(2)
+    g_block(1, 0)
     h_start(1)
-    g_relay(1, (0, 1, 2, 3))
-    h_start(3)
-    g_far(0)
-    h_block(0)
-    g_block(1, 0)
-    h_relay(2)
-    h_relay(1)
-    g_near(0)
+    g_relay(1, (3,))
+    g_relay(1, (2,))
     z_out(0)
     z_out(1)
+    g_block(0, 2)
+    h_start(3)
+    h_relay(2)
+    g_far(0, (0,))
+    g_far(0, (1,))
+    h_block(0)
+    g_block(0, 1)
+    g_block(0, 3)
+    g_near(0, (0,))
+    g_near(0, (1,))
+    h_finish(2)
+    h_relay(1)
+    z_out(3)
+    z_out(2)
+    g_far(0, (3,))
+    g_far(0, (2,))
+    g_relay(0, (0,))
+    g_relay(0, (1,))
     h_relay(3)
-    z_out(2)
-    z_out(3)
-    h_finish(2)
     h_finish(1)
+    g_near(0, (3,))
+    g_near(0, (2,))
+    h_finish(3)
     g_block(0, 0)
     h_start(0)
-    h_finish(3)
-    z_pass(0)
-    z_pass(1)
-    g_relay(0, (0, 1, 2, 3))
+    g_relay(0, (3,))
+    g_relay(0, (2,))
     h_relay(0)
-    z_pass(2)
-    z_pass(3)
     total = h_sum(0)
     for f in (1, 3, 2):
         arrived(("hz", f), hz.at[f])
         total = total + hz[f].astype(F32)
-    go_ref[...] = total
-    for t in range(4):
+    for i in range(2):
+        for half in range(2):
+            at = i * 256 + half * 128
+            go_ref[pl.ds(half * 2 + i, 112, stride=4), :] = total[:, at:at + 128]
+    for t in ORDER:
         part = g_sum(0, t)
-        arrived(("z3", t), zs2.at[t])
-        gp_ref[t] = part + zs2[t].astype(F32)
-    for copy in started:
-        copy.wait_send()
+        arrived(("z2", t), zs2.at[t])
+        part = part + zs2[t].astype(F32)
+        for q in range(4):
+            gp_ref[pl.ds(t * 448 + q, 112, stride=4), :] = part[:, q * 128:(q + 1) * 128]
+    for name in list(started):
+        sent(name)
+
+
+def hand_over(go_in, gp_in, go_out, gp_out):
+    go_out[...] = go_in[...]
+    gp_out[...] = gp_in[...]
 
 
 def per_device(occ_slab, pair_slab, occ_energy, pair_energy, vir_energy):
@@ -373,13 +433,16 @@
     chunk = (112, 512)
     gamma_occ, gamma_pair = pl.pallas_call(
         kernel,
-        out_shape=(jax.ShapeDtypeStruct(chunk, F32), jax.ShapeDtypeStruct((4,) + chunk, F32)),
+        out_shape=(jax.ShapeDtypeStruct((448, 128), F32), jax.ShapeDtypeStruct((1792, 128), F32)),
         in_specs=[vmem, vmem, smem, smem, vmem],
         out_specs=(vmem, vmem),
         scratch_shapes=[
+            pltpu.VMEM((112, 2, 256), F32),
+            pltpu.VMEM((4, 448, 128), F32),
+            pltpu.VMEM(chunk, BF),
+            pltpu.VMEM((8, 56, 512), BF),
             pltpu.VMEM((8, 56, 512), BF),
             pltpu.VMEM((16, 2) + chunk, BF),
-            pltpu.VMEM((4,) + chunk, BF),
             pltpu.VMEM((32,) + chunk, BF),
             pltpu.VMEM((256, 128), F32),
             pltpu.VMEM((512, 512), F32),
@@ -389,7 +452,6 @@
             pltpu.VMEM((2, 4) + chunk, BF),
             pltpu.VMEM((2, 4) + chunk, BF),
             pltpu.VMEM((2, 4) + chunk, BF),
-            pltpu.VMEM((4,) + chunk, BF),
             pltpu.VMEM((4,) + chunk, BF),
             pltpu.VMEM((4, 4) + chunk, F32),
             pltpu.VMEM((4, 4) + chunk, BF),
@@ -407,13 +469,21 @@
         ),
         cost_estimate=pl.CostEstimate(flops=5_600_000_000, bytes_accessed=2_000_000, transcendentals=0),
     )(
-        occ_slab.reshape(chunk),
-        jnp.swapaxes(pair_slab, 0, 1),
+        occ_slab,
+        pair_slab,
         occ_energy,
         pair_energy,
         vir_energy.reshape(1, -1),
     )
-    return gamma_occ.reshape(112, 2, 256), gamma_pair.reshape(448, 1, 512)
+    gamma_occ, gamma_pair = pl.pallas_call(
+        hand_over,
+        grid=(2,),
+        out_shape=(jax.ShapeDtypeStruct((448, 128), F32), jax.ShapeDtypeStruct((1792, 128), F32)),
+        in_specs=[pl.BlockSpec((224, 128), lambda i: (i, 0)), pl.BlockSpec((896, 128), lambda i: (i, 0))],
+        out_specs=(pl.BlockSpec((224, 128), lambda i: (i, 0)), pl.BlockSpec((896, 128), lambda i: (i, 0))),
+    )(gamma_occ, gamma_pair)
+    halves = jnp.swapaxes(gamma_occ.reshape(112, 2, 2, 128), 1, 2)
+    return halves.reshape(112, 2, 256), gamma_pair.reshape(448, 1, 512)
 
 
 def solution(mesh):

time: 112 us -> 99.6 us (0.89)
  the two profiles are of different devices: /device:TPU:64 before, /device:TPU:1 now
where the time goes in v3:
time: 99.6 us; the launch traced here: 99 us
  Pallas kernels  97.8 us (98%)
  between operations  1.28 us (1%)
    pallas_call x1, Pallas kernels, per_device(): pl.pallas_call(kernel, out_shape=(jax.ShapeDtypeStruct((448, 128), F32),...  95.6 us
    pallas_call x1, Pallas kernels, per_device(): pl.pallas_call(hand_over, grid=(2,), out_shape=(jax.ShapeDtypeStruct((448...  2.13 us

profile of v3, /device:TPU:1, one launch (start us, length us, event | category | flops | bytes accessed | tf_op | source)
XLA Modules:
  0.0 99.0 jit_solution(3029105091487976139)
XLA Ops:
  1.3 95.6 %shard_map.68 = (f32[448,128]{1,0:T(8,128)}, f32[1792,128]{1,0:T(8,128)}) custom-call(bf16[112,2,256]{2,1,0:T(2,128)(2,1)} %occ_raw.1, bf16[56,8,512]{2,1,0:T(8,128)(2,1)} %pair_raw.1, f32[2]{0:T(128)} %eo_ref.1, f32[1]{0:T(128)S(6)} %copy.9.ep_ref, f32[1,2048]{1,0:T(1,128)} %bitcast.9), custom_call_target="tpu_custom_call" | custom-call | flops 5600000000 | bytes 2000000 | tf_op jit(solution)/shard_map/pallas_call | solution.py:434
  96.9 2.1 %shard_map.69 = (f32[448,128]{1,0:T(8,128)}, f32[1792,128]{1,0:T(8,128)}) custom-call(f32[448,128]{1,0:T(8,128)} %get-tuple-element.6.go_in, f32[1792,128]{1,0:T(8,128)} %get-tuple-element.7.gp_in), custom_call_target="tpu_custom_call" | custom-call | tf_op jit(solution)/shard_map/pallas_call | solution.py:478

commit v4 on v3

--- a/solution.py
+++ b/solution.py
@@ -9,8 +9,8 @@
 BF = jnp.bfloat16
 F32 = jnp.float32
 ORDER = (0, 1, 3, 2)
-PAIR_DIRECT = ((1, 2),)
-OCC_DIRECT = (3,)
+PAIR_DIRECT = ()
+OCC_DIRECT = ()
 PLUS = (0, 3)
 
 
@@ -95,8 +95,6 @@
     for j in range(8):
         for q in range(4):
             pair_ref[j, :, q * 128:(q + 1) * 128] = pair_wide[q, pl.ds(j, 56, stride=8), :].astype(BF)
-    occ_wide[...] = occ_raw[...].astype(F32)
-    occ_ref[...] = jnp.concatenate([occ_wide[:, 0, :], occ_wide[:, 1, :]], axis=1).astype(BF)
     pl.semaphore_wait(barrier, len(partners))
 
     def pblk(h, yy, xx):
@@ -113,9 +111,16 @@
     def oblk(f, dx, sib=False):
         return occs.at[zsrc(f) * 8 + ((x + dx) % 4) * 2 + (other_c if sib else c)]
 
-    for dx, dc in ((0, True), (1, False), (1, True), (3, False), (3, True), (2, False), (2, True)):
-        dev = at_x(dx, dc)
-        send(("s1", dx, dc), pair_ref.at[dev["oj"]], stage.at[dx * 2 + int(dc)], dev)
+    def pair_out(dx):
+        for dc in (False, True):
+            if dx or dc:
+                dev = at_x(dx, dc)
+                send(("s1", dx, dc), pair_ref.at[dev["oj"]], stage.at[dx * 2 + int(dc)], dev)
+
+    for dx in (0, 1, 3):
+        pair_out(dx)
+    occ_wide[...] = occ_raw[...].astype(F32)
+    occ_ref[...] = jnp.concatenate([occ_wide[:, 0, :], occ_wide[:, 1, :]], axis=1).astype(BF)
     own_rows = occs.at[vb * 8 + oj]
 
     oz_at = {f: rsem.index(("oz", f)) for f in (1, 2, 3)}
@@ -210,6 +215,21 @@
         arrived(("oF", f), far)
         send(("oS", 3, f), far, far, at_x(0, True))
 
+    def occ_all(f):
+        for m, dx in ((0, 0), (1, 3), (2, 1), (3, 2)):
+            arrived(("oS", m, f), oblk(f, dx, True))
+
+    def pair_far(h, e):
+        arrived(("yF", h, e), pblk(h, (y + 2) % 4, xs(e)))
+
+    def t_add(h, dy):
+        hh = zh if h == 0 else 1 - zh
+        group = hh * 4 + (y + dy) % 4
+        a = occs[pl.ds(group * 4, 4)].reshape(448, 512)
+        b = pairs[pl.ds(group * 2, 2)].reshape(448, 512)
+        tacc[...] += dot(a, b, 0, 0)
+
+    pair_out(2)
     occ_out(2)
     pair_merge(0)
     z_out1(0)
@@ -231,44 +251,40 @@
     occ_forward(0)
     sent(("zf", 1))
     z_out1(2)
+    occ_forward(2)
     z_in(1)
+    occ_forward(1)
     y_forward(1, 0)
-    occ_forward(2)
+    occ_far(0)
+    occ_forward(3)
     z_in(3)
-    occ_forward(1)
-    occ_far(0)
+    occ_far(2)
+    occ_far(1)
     y_forward(1, 1)
+    occ_far(3)
+    pair_far(0, 0)
+    pair_far(0, 1)
+    pair_far(0, 3)
+    pair_far(0, 2)
     z_in(2)
-    occ_forward(3)
-    occ_far(2)
-    y_forward(1, 3)
-    occ_far(1)
-    occ_far(3)
-    y_forward(1, 2)
-    for f in ORDER:
-        for m, dx in ((0, 0), (1, 3), (2, 1), (3, 2)):
-            arrived(("oS", m, f), oblk(f, dx, True))
-
-    def t_add(h, dy):
-        hh = zh if h == 0 else 1 - zh
-        group = hh * 4 + (y + dy) % 4
-        a = occs[pl.ds(group * 4, 4)].reshape(448, 512)
-        b = pairs[pl.ds(group * 2, 2)].reshape(448, 512)
-        tacc[...] += dot(a, b, 0, 0)
-
+    occ_all(0)
+    occ_all(1)
+    occ_all(3)
+    occ_all(2)
     t_add(0, 0)
     t_add(0, 1)
     t_add(0, 3)
+    t_add(0, 2)
     t_add(1, 0)
-    for e in ORDER:
-        arrived(("yF", 0, e), pblk(0, (y + 2) % 4, xs(e)))
-    t_add(0, 2)
+    y_forward(1, 3)
+    y_forward(1, 2)
     t_add(1, 1)
     t_add(1, 3)
-    for e in ORDER:
-        arrived(("yF", 1, e), pblk(1, (y + 2) % 4, xs(e)))
+    pair_far(1, 0)
+    pair_far(1, 1)
+    pair_far(1, 3)
+    pair_far(1, 2)
     t_add(1, 2)
-
     vb_row = vir_ref[:, pl.ds(pl.multiple_of(vb * 512, 512), 512)]
     va_cols = jnp.concatenate([ecol[...]] * 4, axis=1)
     for i in range(2):

time: 99.6 us -> 99.4 us (level)
  no operation moved by 1% of the time
where the time goes in v4:
time: 99.4 us; the launch traced here: 99 us
  Pallas kernels  97.7 us (98%)
  between operations  1.28 us (1%)
    pallas_call x1, Pallas kernels, per_device(): pl.pallas_call(kernel, out_shape=(jax.ShapeDtypeStruct((448, 128), F32),...  95.6 us
    pallas_call x1, Pallas kernels, per_device(): pl.pallas_call(hand_over, grid=(2,), out_shape=(jax.ShapeDtypeStruct((448...  2.13 us

profile of v4, /device:TPU:1, one launch (start us, length us, event | category | flops | bytes accessed | tf_op | source)
XLA Modules:
  0.0 99.0 jit_solution(17338109116237193678)
XLA Ops:
  1.3 95.6 %shard_map.68 = (f32[448,128]{1,0:T(8,128)}, f32[1792,128]{1,0:T(8,128)}) custom-call(bf16[112,2,256]{2,1,0:T(2,128)(2,1)} %occ_raw.1, bf16[56,8,512]{2,1,0:T(8,128)(2,1)} %pair_raw.1, f32[2]{0:T(128)} %eo_ref.1, f32[1]{0:T(128)S(6)} %copy.9.ep_ref, f32[1,2048]{1,0:T(1,128)} %bitcast.9), custom_call_target="tpu_custom_call" | custom-call | flops 5600000000 | bytes 2000000 | tf_op jit(solution)/shard_map/pallas_call | solution.py:450
  96.9 2.1 %shard_map.69 = (f32[448,128]{1,0:T(8,128)}, f32[1792,128]{1,0:T(8,128)}) custom-call(f32[448,128]{1,0:T(8,128)} %get-tuple-element.6.go_in, f32[1792,128]{1,0:T(8,128)} %get-tuple-element.7.gp_in), custom_call_target="tpu_custom_call" | custom-call | tf_op jit(solution)/shard_map/pallas_call | solution.py:494

commit v5 on v4

--- a/solution.py
+++ b/solution.py
@@ -420,6 +420,9 @@
     g_relay(0, (3,))
     g_relay(0, (2,))
     h_relay(0)
+    for name in list(started):
+        if name[0] not in ("gR", "gL", "z2", "hz", "hR", "hL"):
+            sent(name)
     total = h_sum(0)
     for f in (1, 3, 2):
         arrived(("hz", f), hz.at[f])
@@ -493,10 +496,9 @@
     )
     gamma_occ, gamma_pair = pl.pallas_call(
         hand_over,
-        grid=(2,),
         out_shape=(jax.ShapeDtypeStruct((448, 128), F32), jax.ShapeDtypeStruct((1792, 128), F32)),
-        in_specs=[pl.BlockSpec((224, 128), lambda i: (i, 0)), pl.BlockSpec((896, 128), lambda i: (i, 0))],
-        out_specs=(pl.BlockSpec((224, 128), lambda i: (i, 0)), pl.BlockSpec((896, 128), lambda i: (i, 0))),
+        in_specs=[vmem, vmem],
+        out_specs=(vmem, vmem),
     )(gamma_occ, gamma_pair)
     halves = jnp.swapaxes(gamma_occ.reshape(112, 2, 2, 128), 1, 2)
     return halves.reshape(112, 2, 256), gamma_pair.reshape(448, 1, 512)

time: 99.4 us -> 99.6 us (level)
  no operation moved by 1% of the time
where the time goes in v5:
time: 99.6 us; the launch traced here: 99.2 us
  Pallas kernels  97.9 us (98%)
  between operations  1.28 us (1%)
    pallas_call x1, Pallas kernels, per_device(): pl.pallas_call(kernel, out_shape=(jax.ShapeDtypeStruct((448, 128), F32),...  95.6 us
    pallas_call x1, Pallas kernels, per_device(): pl.pallas_call(hand_over, out_shape=(jax.ShapeDtypeStruct((448, 128), F32...  2.32 us

profile of v5, /device:TPU:1, one launch (start us, length us, event | category | flops | bytes accessed | tf_op | source)
XLA Modules:
  0.0 99.2 jit_solution(15533550840027114932)
XLA Ops:
  1.3 95.6 %shard_map.68 = (f32[448,128]{1,0:T(8,128)}, f32[1792,128]{1,0:T(8,128)}) custom-call(bf16[112,2,256]{2,1,0:T(2,128)(2,1)} %occ_raw.1, bf16[56,8,512]{2,1,0:T(8,128)(2,1)} %pair_raw.1, f32[2]{0:T(128)} %eo_ref.1, f32[1]{0:T(128)S(6)} %copy.9.ep_ref, f32[1,2048]{1,0:T(1,128)} %bitcast.9), custom_call_target="tpu_custom_call" | custom-call | flops 5600000000 | bytes 2000000 | tf_op jit(solution)/shard_map/pallas_call | solution.py:453
  96.9 2.3 %shard_map.69 = (f32[448,128]{1,0:T(8,128)}, f32[1792,128]{1,0:T(8,128)}) custom-call(f32[448,128]{1,0:T(8,128)} %get-tuple-element.6.go_in, f32[1792,128]{1,0:T(8,128)} %get-tuple-element.7.gp_in), custom_call_target="tpu_custom_call" | custom-call | tf_op jit(solution)/shard_map/pallas_call | solution.py:497
